TPU v7x, 256 devices: a whole 4x4x8 slice. The times are simulated.
256 devices in a mesh: cuts: 2 (over z_lo), dev: 128 (over y, z_hi, x, core).
Axes of the slice: x: 4, y: 4, z: 8 (z_hi: 4, z_lo: 2; z = z_hi * 2 + z_lo), core: 2. Of those that a mesh axis runs over, the one named last changes fastest.
Arguments:
- resp_q: bfloat16 [131072, 2048], P(('cuts', 'dev')), may hold values from -64 to 64, as said below
- resp_kv: bfloat16 [131072, 1024], P(('cuts', 'dev')), may hold values from -6 to 6
- resp_out_grad: bfloat16 [131072, 2048], P(('cuts', 'dev')), may hold values from -6 to 6
- resp_x: bfloat16 [131072, 4096], P(('cuts', 'dev')), may hold values from -24 to 24
- prompt_kv: bfloat16 [32768, 1024], P(('cuts', 'dev')), may hold values from -6 to 6
- stretch_offset: int32 [2048], P(('cuts', 'dev')), may hold values from -2 to 2
Outputs:
- prompt_kv_grad: float32 [32768, 1024], P(('cuts', 'dev'))
- kv_weight_grad: float32 [4096, 1024], P('dev')
Inputs may be any that keep to these rules, and one draw needn't show every extreme that they name: `stretch_offset`: each entry lies between -2 and 2; counts per prompt are uneven. `resp_q`: queries are real-valued; a few rows are much larger than the rest.
All inputs are finite; a program needn't handle non-finite values.
Results may differ from a plain program's by a relative error of at most 0.012.
Values may be sent and summed in bfloat16 or wider, within the bound.
A program may use at most 128 MiB of HBM per device.

v0:
```python
import jax
import jax.numpy as jnp
from jax import lax
from jax.sharding import PartitionSpec as P

QH = 16
KVH = 4
HD = 128
PLEN = 128
STRETCH = 64
REACH = 2
KVW = 1024


def from_behind(value, axis, steps):
    count = lax.axis_size(axis)
    pairs = [(source, (source + steps) % count) for source in range(count)]
    return lax.ppermute(value, axis, pairs)


def block_terms(queries, own_kv, out_grad, chosen):
    count = queries.shape[0]
    group = QH // KVH
    half = KVH * HD
    span = PLEN + STRETCH
    keys = jnp.concatenate([chosen[:, :, :half], own_kv[:, :, :half]], axis=1).reshape(
        count, span, KVH, HD
    )
    values = jnp.concatenate([chosen[:, :, half:], own_kv[:, :, half:]], axis=1).reshape(
        count, span, KVH, HD
    )
    qq = queries.reshape(count, STRETCH, KVH, group, HD)
    dout = out_grad.reshape(count, STRETCH, KVH, group, HD)
    scale = HD ** (-0.5)
    scores = jnp.einsum("cikgd,cjkd->ckgij", qq, keys, preferred_element_type=jnp.float32) * scale
    keypos = jnp.arange(span)
    qpos = jnp.arange(STRETCH)
    visible = (keypos[None, :] < PLEN) | (keypos[None, :] - PLEN <= qpos[:, None])
    scores = jnp.where(visible, scores, -1e30)
    top = jnp.max(scores, axis=-1, keepdims=True)
    expo = jnp.exp(scores - top)
    probs = expo / jnp.sum(expo, axis=-1, keepdims=True)
    probs_b = probs.astype(jnp.bfloat16)
    out = jnp.einsum("ckgij,cjkd->cikgd", probs_b, values, preferred_element_type=jnp.float32)
    rowdot = jnp.sum(dout.astype(jnp.float32) * out, axis=-1)
    dprobs = jnp.einsum("cikgd,cjkd->ckgij", dout, values, preferred_element_type=jnp.float32)
    dscores = probs * (dprobs - jnp.transpose(rowdot, (0, 2, 3, 1))[..., None])
    dscores_b = dscores.astype(jnp.bfloat16)
    kgrad = (
        jnp.einsum("ckgij,cikgd->cjkd", dscores_b, qq, preferred_element_type=jnp.float32) * scale
    )
    vgrad = jnp.einsum("ckgij,cikgd->cjkd", probs_b, dout, preferred_element_type=jnp.float32)
    return jnp.concatenate(
        [kgrad.reshape(count, span, half), vgrad.reshape(count, span, half)], axis=-1
    )


def single_block(items):
    queries, own_kv, out_grad, chosen = items
    return block_terms(queries[None], own_kv[None], out_grad[None], chosen[None])[0]


def shards(resp_q, resp_kv, resp_out_grad, resp_x, prompt_kv, stretch_offset):
    count = resp_q.shape[0] // STRETCH
    moves = [step_by for step_by in range(1, REACH + 1)] + [
        0 - step_by for step_by in range(1, REACH + 1)
    ]
    gathered = [prompt_kv]
    for step_by in moves:
        gathered.append(from_behind(prompt_kv, "dev", step_by))
    stacked = jnp.stack(gathered)
    position = jnp.where(stretch_offset >= 0, stretch_offset, REACH - stretch_offset)
    chosen = jnp.take(stacked, position, axis=0)
    terms = lax.map(
        single_block,
        (
            resp_q.reshape(count, STRETCH, QH * HD),
            resp_kv.reshape(count, STRETCH, KVW),
            resp_out_grad.reshape(count, STRETCH, QH * HD),
            chosen,
        ),
    )
    resp_grad_b = terms[:, PLEN:].reshape(count * STRETCH, KVW).astype(jnp.bfloat16)
    weight_local = lax.dot_general(
        resp_x, resp_grad_b, (((0,), (0,)), ((), ())), preferred_element_type=jnp.float32
    )
    selector = (position[:, None] == jnp.arange(2 * REACH + 1)[None, :]).astype(jnp.float32)
    by_owner = jnp.einsum("cn,cpw->npw", selector, terms[:, :PLEN])
    prompt_kv_grad = by_owner[0]
    for index, step_by in enumerate(moves):
        prompt_kv_grad = prompt_kv_grad + from_behind(by_owner[index + 1], "dev", 0 - step_by)
    shared = lax.psum_scatter(weight_local, "dev", scatter_dimension=0, tiled=True)
    kv_weight_grad = lax.psum(shared, "cuts")
    return (prompt_kv_grad, kv_weight_grad)


def solution(mesh):
    return jax.shard_map(
        shards,
        mesh=mesh,
        in_specs=(
            P(("cuts", "dev"), None),
            P(("cuts", "dev"), None),
            P(("cuts", "dev"), None),
            P(("cuts", "dev"), None),
            P(("cuts", "dev"), None),
            P(("cuts", "dev")),
        ),
        out_specs=(P(("cuts", "dev"), None), P("dev", None)),
        check_vma=False,
    )
```

profile of v0, /device:TPU:1, one launch (start us, length us, event | category | flops | bytes accessed | tf_op | source)
XLA Modules:
  0.0 1039.4 jit_solution(4523339180805699223)
XLA Ops:
  7.2 2.1 collective-permute-start.1
  9.3 2.1 collective-permute-start
  11.4 7.6 collective-permute-start.3
  19.0 1.0 collective-permute-start.2
  19.9 1.0 bitcast_dynamic-update-slice_fusion.4
  21.6 5.0 collective-permute-done.1
  26.7 5.3 collective-permute-done.3
  32.7 1.6 broadcast_select_fusion
  34.3 183.1 %while.12 = (s32[]{:T(128)}, bf16[8,192,1024]{2,0,1:T(8,128)(2,1)}, bf16[8,64,2048]{2,1,0:T(8,128)(2,1)}, bf16[8,128,1024]{2,1,0:T(8,128)(2,1)}, bf16[8,64,1024]...) while((s32[]{:T(128)}, bf16[8,192,1024]{2,0,1:T(8,128)(2,1)}, ...), condition=%wide.region_4.5_spmd, body=%wide.region_0.4_spmd.sunk | while | flops 256169344 | bytes 16119817 | solution.py:74
  34.3 0.9 constant_dynamic-slice_fusion.10
  35.2 1.0 constant_dynamic-slice_fusion.11
  36.4 1.1 constant_dynamic-slice_fusion.9
  42.2 15.0 %dynamic_update_slice.8 = bf16[8,192,1024]{2,0,1:T(8,128)(2,1)} dynamic-update-slice(bf16[8,192,1024]{2,0,1:T(8,128)(2,1)} %get-tuple-element.196, bf16[1,192,1024]{2,0,1:T(2,128)(2,1)S(1)} %pad_maximum_fusion.6, s32[]{:T(128)S(6)} %copy.151, s32[]{:T(128)} %constant.68.clone.1..sunk, s32[]{:T(128)} %constant.68.clone.1..sunk) | dynamic-update-slice | bytes 786436 | tf_op jit(solution)/shard_map/while/body/jit(dynamic_update_index_in_dim)/dynamic_update_slice | solution.py:74
  58.1 1.0 constant_dynamic-slice_fusion.11
  59.2 1.1 constant_dynamic-slice_fusion.9
  65.1 15.0 %dynamic_update_slice.8 = bf16[8,192,1024]{2,0,1:T(8,128)(2,1)} dynamic-update-slice(bf16[8,192,1024]{2,0,1:T(8,128)(2,1)} %get-tuple-element.196, bf16[1,192,1024]{2,0,1:T(2,128)(2,1)S(1)} %pad_maximum_fusion.6, s32[]{:T(128)S(6)} %copy.151, s32[]{:T(128)} %constant.68.clone.1..sunk, s32[]{:T(128)} %constant.68.clone.1..sunk) | dynamic-update-slice | bytes 786436 | tf_op jit(solution)/shard_map/while/body/jit(dynamic_update_index_in_dim)/dynamic_update_slice | solution.py:74
  81.0 1.0 constant_dynamic-slice_fusion.11
  82.1 1.1 constant_dynamic-slice_fusion.9
  87.9 15.0 %dynamic_update_slice.8 = bf16[8,192,1024]{2,0,1:T(8,128)(2,1)} dynamic-update-slice(bf16[8,192,1024]{2,0,1:T(8,128)(2,1)} %get-tuple-element.196, bf16[1,192,1024]{2,0,1:T(2,128)(2,1)S(1)} %pad_maximum_fusion.6, s32[]{:T(128)S(6)} %copy.151, s32[]{:T(128)} %constant.68.clone.1..sunk, s32[]{:T(128)} %constant.68.clone.1..sunk) | dynamic-update-slice | bytes 786436 | tf_op jit(solution)/shard_map/while/body/jit(dynamic_update_index_in_dim)/dynamic_update_slice | solution.py:74
  103.9 1.0 constant_dynamic-slice_fusion.11
  105.0 1.1 constant_dynamic-slice_fusion.9
  110.8 15.0 %dynamic_update_slice.8 = bf16[8,192,1024]{2,0,1:T(8,128)(2,1)} dynamic-update-slice(bf16[8,192,1024]{2,0,1:T(8,128)(2,1)} %get-tuple-element.196, bf16[1,192,1024]{2,0,1:T(2,128)(2,1)S(1)} %pad_maximum_fusion.6, s32[]{:T(128)S(6)} %copy.151, s32[]{:T(128)} %constant.68.clone.1..sunk, s32[]{:T(128)} %constant.68.clone.1..sunk) | dynamic-update-slice | bytes 786436 | tf_op jit(solution)/shard_map/while/body/jit(dynamic_update_index_in_dim)/dynamic_update_slice | solution.py:74
  126.8 1.0 constant_dynamic-slice_fusion.11
  127.9 1.1 constant_dynamic-slice_fusion.9
  133.7 15.0 %dynamic_update_slice.8 = bf16[8,192,1024]{2,0,1:T(8,128)(2,1)} dynamic-update-slice(bf16[8,192,1024]{2,0,1:T(8,128)(2,1)} %get-tuple-element.196, bf16[1,192,1024]{2,0,1:T(2,128)(2,1)S(1)} %pad_maximum_fusion.6, s32[]{:T(128)S(6)} %copy.151, s32[]{:T(128)} %constant.68.clone.1..sunk, s32[]{:T(128)} %constant.68.clone.1..sunk) | dynamic-update-slice | bytes 786436 | tf_op jit(solution)/shard_map/while/body/jit(dynamic_update_index_in_dim)/dynamic_update_slice | solution.py:74
  148.8 0.9 constant_dynamic-slice_fusion.10
  149.7 1.0 constant_dynamic-slice_fusion.11
  150.8 1.1 constant_dynamic-slice_fusion.9
  156.6 15.0 %dynamic_update_slice.8 = bf16[8,192,1024]{2,0,1:T(8,128)(2,1)} dynamic-update-slice(bf16[8,192,1024]{2,0,1:T(8,128)(2,1)} %get-tuple-element.196, bf16[1,192,1024]{2,0,1:T(2,128)(2,1)S(1)} %pad_maximum_fusion.6, s32[]{:T(128)S(6)} %copy.151, s32[]{:T(128)} %constant.68.clone.1..sunk, s32[]{:T(128)} %constant.68.clone.1..sunk) | dynamic-update-slice | bytes 786436 | tf_op jit(solution)/shard_map/while/body/jit(dynamic_update_index_in_dim)/dynamic_update_slice | solution.py:74
  172.6 1.0 constant_dynamic-slice_fusion.11
  173.7 1.1 constant_dynamic-slice_fusion.9
  179.5 15.0 %dynamic_update_slice.8 = bf16[8,192,1024]{2,0,1:T(8,128)(2,1)} dynamic-update-slice(bf16[8,192,1024]{2,0,1:T(8,128)(2,1)} %get-tuple-element.196, bf16[1,192,1024]{2,0,1:T(2,128)(2,1)S(1)} %pad_maximum_fusion.6, s32[]{:T(128)S(6)} %copy.151, s32[]{:T(128)} %constant.68.clone.1..sunk, s32[]{:T(128)} %constant.68.clone.1..sunk) | dynamic-update-slice | bytes 786436 | tf_op jit(solution)/shard_map/while/body/jit(dynamic_update_index_in_dim)/dynamic_update_slice | solution.py:74
  194.6 0.9 constant_dynamic-slice_fusion.10
  195.5 1.0 constant_dynamic-slice_fusion.11
  196.6 1.1 constant_dynamic-slice_fusion.9
  202.4 15.0 %dynamic_update_slice.8 = bf16[8,192,1024]{2,0,1:T(8,128)(2,1)} dynamic-update-slice(bf16[8,192,1024]{2,0,1:T(8,128)(2,1)} %get-tuple-element.196, bf16[1,192,1024]{2,0,1:T(2,128)(2,1)S(1)} %pad_maximum_fusion.6, s32[]{:T(128)S(6)} %copy.151, s32[]{:T(128)} %constant.68.clone.1..sunk, s32[]{:T(128)} %constant.68.clone.1..sunk) | dynamic-update-slice | bytes 786436 | tf_op jit(solution)/shard_map/while/body/jit(dynamic_update_index_in_dim)/dynamic_update_slice | solution.py:74
  217.4 3.8 copy.61
  221.3 8.2 convolution_bitcast_fusion.4
  229.5 17.4 %copy.74 = f32[4096,1024]{1,0:T(8,128)} copy(f32[4096,1024]{0,1:T(8,128)} %convolution_bitcast_fusion.4) | data formatting | bytes 33554432
  247.6 1.2 copy-done
  249.5 2.0 fusion.37
  252.1 5.2 collective-permute-start.4
  257.3 8.0 collective-permute-start.5
  265.3 719.7 %reduce-scatter.4.cloned.1.call-done = f32[32,1024]{1,0:T(8,128)} async-done(((f32[4096,1024]{1,0:T(8,128)}), f32[32,1024]{1,0:T(8,128)}) %reduce-scatter.4.cloned.1.call-update) | async-done | bytes 131088
  985.0 1.9 copy.75
  987.0 2.4 fusion.32
  989.4 41.2 %all-reduce.2.cloned.1.call-done = f32[32,1024]{0,1:T(8,128)} async-done(((f32[32,1024]{0,1:T(8,128)}), f32[32,1024]{0,1:T(8,128)}) %all-reduce.2.cloned.1.call-update) | async-done | bytes 131088 | tf_op jit(solution)/shard_map/psum | solution.py:93
  1030.7 1.9 copy.62
  (181 shorter events, 46.6 us)
Async XLA Ops:
  7.2 977.9 %reduce-scatter.4.cloned.1.call-start = ((), (), s32[]{:S(2)}) async-start(), calls=%async_computation.2 | async-start | bytes 16908288
  7.2 19.4 %collective-permute-start.1 = (bf16[128,1024]{1,0:T(8,128)(2,1)}, bf16[128,1024]{1,0:T(8,128)(2,1)S(1)}, u32[]{:S(2)}, u32[]{:S(2)}) collective-permute-start(bf16[128,1024]{1,0:T(8,128)(2,1)} %param.12), channel_id=1, source_target_pairs={{0,2},{1,3},{2,4},{3,5},{4,6},{5,7},{6,8},{7,9},{8,10},{9,11},{10,... | collective-permute-start | bytes 786440 | tf_op jit(solution)/shard_map/ppermute | solution.py:18
  9.3 12.2 %collective-permute-start = (bf16[128,1024]{1,0:T(8,128)(2,1)}, bf16[128,1024]{1,0:T(8,128)(2,1)S(1)}, u32[]{:S(2)}, u32[]{:S(2)}) collective-permute-start(bf16[128,1024]{1,0:T(8,128)(2,1)} %param.12), channel_id=1, source_target_pairs={{0,1},{1,2},{2,3},{3,4},{4,5},{5,6},{6,7},{7,8},{8,9},{9,10},{10,1... | collective-permute-start | bytes 786440 | tf_op jit(solution)/shard_map/ppermute | solution.py:18
  11.4 20.6 %collective-permute-start.3 = (bf16[128,1024]{1,0:T(8,128)(2,1)}, bf16[128,1024]{1,0:T(8,128)(2,1)S(1)}, u32[]{:S(2)}, u32[]{:S(2)}) collective-permute-start(bf16[128,1024]{1,0:T(8,128)(2,1)} %param.12), channel_id=1, source_target_pairs={{0,126},{1,127},{2,0},{3,1},{4,2},{5,3},{6,4},{7,5},{8,6},{9,7},{1... | collective-permute-start | bytes 786440 | tf_op jit(solution)/shard_map/ppermute | solution.py:18
  19.0 7.7 collective-permute-start.2
  217.4 3.8 copy-start.1
  246.9 0.7 copy-start.2
  246.9 1.9 copy-start
  247.0 783.7 %all-reduce.2.cloned.1.call-start = ((), (), s32[]{:S(2)}) async-start(), calls=%async_computation.1 | async-start | bytes 1048576 | tf_op jit(solution)/shard_map/psum | solution.py:93
  251.9 735.0 %collective-permute-start.6 = (f32[128,1024]{1,0:T(8,128)S(1)}, f32[128,1024]{1,0:T(8,128)S(1)}, u32[]{:S(2)}, u32[]{:S(2)}) collective-permute-start(f32[128,1024]{1,0:T(8,128)S(1)} %bitcast.149), channel_id=1, source_target_pairs={{0,1},{1,2},{2,3},{3,4},{4,5},{5,6},{6,7},{7,8},{8,9},{9,10},{10,1... | collective-permute-start | bytes 1572872 | tf_op jit(solution)/shard_map/ppermute | solution.py:18
  252.0 735.0 %collective-permute-start.7 = (f32[128,1024]{1,0:T(8,128)S(1)}, f32[128,1024]{1,0:T(8,128)}, u32[]{:S(2)}, u32[]{:S(2)}) collective-permute-start(f32[128,1024]{1,0:T(8,128)S(1)} %bitcast.148), channel_id=1, source_target_pairs={{0,2},{1,3},{2,4},{3,5},{4,6},{5,7},{6,8},{7,9},{8,10},{9,11},{10,... | collective-permute-start | bytes 1572872 | tf_op jit(solution)/shard_map/ppermute | solution.py:18
  252.1 734.9 %collective-permute-start.4 = (f32[128,1024]{1,0:T(8,128)S(1)}, f32[128,1024]{1,0:T(8,128)}, u32[]{:S(2)}, u32[]{:S(2)}) collective-permute-start(f32[128,1024]{1,0:T(8,128)S(1)} %bitcast.147), channel_id=1, source_target_pairs={{0,127},{1,0},{2,1},{3,2},{4,3},{5,4},{6,5},{7,6},{8,7},{9,8},{10,... | collective-permute-start | bytes 1572872 | tf_op jit(solution)/shard_map/ppermute | solution.py:18
  257.3 729.7 %collective-permute-start.5 = (f32[128,1024]{1,0:T(8,128)S(1)}, f32[128,1024]{1,0:T(8,128)}, u32[]{:S(2)}, u32[]{:S(2)}) collective-permute-start(f32[128,1024]{1,0:T(8,128)S(1)} %bitcast.146), channel_id=1, source_target_pairs={{0,126},{1,127},{2,0},{3,1},{4,2},{5,3},{6,4},{7,5},{8,6},{9,7},{1... | collective-permute-start | bytes 1572872 | tf_op jit(solution)/shard_map/ppermute | solution.py:18
Sparse Core Ops, SparseCore 0:
  247.1 737.9 reduce-scatter.3
  987.6 42.9 all-reduce.1
where the time goes:
time: 1040 us
  waiting for transfers between devices  771 us (74%)
  local copies, waits for them, and re-layouts  185 us (18%)
  starting transfers between devices  26.4 us (3%)
  matrix products  24.7 us (2%)
  other arithmetic  16.7 us (2%)
  between operations  14.2 us (1%)
    unnamed x3, waiting for transfers between devices  720 us
    dynamic_update_slice x8, local copies, waits for them, and re-layouts, shards(): lax.map(single_block, (resp_q.reshape(count, STRETCH, QH * HD), resp_kv.r...  120 us
    psum x1, waiting for transfers between devices, shards(): kv_weight_grad = lax.psum(shared, 'cuts')  41.2 us
    ppermute x8, starting transfers between devices, from_behind(): return lax.ppermute(value, axis, pairs)  26.1 us
    unnamed x17, local copies, waits for them, and re-layouts  24.2 us
  transfers between devices with their start and end apart: 10, of which 4 were waited for; matrix products, arithmetic and copies ran while one was open for 1% of the time, Pallas kernels for 0%

commit v1 on v0

v1 whole, which is shorter than its diff:
```python
import math

import jax
import jax.numpy as jnp
from jax import lax
from jax.experimental import pallas as pl
from jax.experimental.pallas import tpu as pltpu
from jax.sharding import PartitionSpec as P

QH = 16
KVH = 4
GROUP = QH // KVH
HD = 128
PLEN = 128
STRETCH = 64
REACH = 2
KVW = 1024
HALF = KVH * HD
BLOCKS = 8
TOK = BLOCKS * STRETCH
RING = 4
TILES = 16
PAIR = 2 * HD
Z_Y = (0, 1, 2)
Z_X = (3,)
ROWS_Y = len(Z_Y) * 128
ROWS_X = len(Z_X) * 128
SHIFT = (0, 1, 2, -1, -2)
SCALE = HD ** -0.5
LOG2E = 1.4426950408889634

BF = jnp.bfloat16
F32 = jnp.float32


def remote(src, dst, send, recv, device):
    return pltpu.make_async_remote_copy(
        src_ref=src,
        dst_ref=dst,
        send_sem=send,
        recv_sem=recv,
        device_id=device,
        device_id_type=pl.DeviceIdType.MESH,
    )


def nt(a, b):
    return lax.dot_general(a, b, (((1,), (1,)), ((), ())), preferred_element_type=F32)


def nn(a, b):
    return lax.dot_general(a, b, (((1,), (0,)), ((), ())), preferred_element_type=F32)


def place_of(x, core):
    same = (x // 2 + core + 1) % 2
    to_x = same * x + (1 - same) * (3 - x)
    to_core = same * (1 - core) + (1 - same) * core
    return to_x, to_core


def source_of(x, core):
    same = (x // 2 + core + 1) % 2
    from_x = (1 - same) * x + same * (3 - x)
    from_core = (1 - same) * (1 - core) + same * core
    return from_x, from_core


def part_of(x, core):
    to_x, to_core = place_of(x, core)
    return (to_x % 2) * 2 + to_core


class Ring:
    def __init__(self, buf, near, full, far_sems, send, mine, right, left, far, to_right, to_left):
        self.buf, self.near, self.full = buf, near, full
        self.recv, self.send = far_sems, send
        self.mine, self.right, self.left, self.far = mine, right, left, far
        self.to_right, self.to_left = to_right, to_left
        self.rows = buf.shape[1]
        self.half = self.rows // 2

    def copy(self, which):
        low, high = pl.ds(0, self.half), pl.ds(self.half, self.half)
        source = (
            self.buf.at[self.far, low],
            self.buf.at[self.far, high],
            self.buf.at[self.right],
            self.buf.at[self.left],
        )[which]
        target = (self.near if which < 2 else self.full).at[which % 2]
        device = (self.to_right, self.to_left)[which % 2]
        return remote(source, target, self.send, self.recv.at[which], device)

    def first(self):
        self.copy(0).start()
        self.copy(1).start()

    def second(self):
        half = self.half
        self.copy(0).wait_recv()
        self.buf[self.right, 0:half] = (
            self.buf[self.right, 0:half].astype(F32) + self.near[0].astype(F32)
        ).astype(BF)
        self.copy(2).start()
        self.copy(1).wait_recv()
        self.buf[self.left, half:] = (
            self.buf[self.left, half:].astype(F32) + self.near[1].astype(F32)
        ).astype(BF)
        self.copy(3).start()

    def arrive(self):
        self.copy(2).wait_recv()
        self.copy(3).wait_recv()

    def total(self, rows):
        return (
            self.buf[self.mine, rows].astype(F32)
            + self.full[0, rows].astype(F32)
            + self.full[1, rows].astype(F32)
        )

    def sent(self):
        whole = self.buf.at[pl.ds(0, 3)]
        remote(whole, whole, self.send, self.recv.at[0], self.to_right).wait_send()


def kernel(
    off_ref, q_hbm, kv_hbm, do_hbm, x_hbm, p_hbm, outp_ref, outw_ref,
    q_v, do_v, kv_v, xo_v, xp_v, xt_v, pk0, pk1, pk2, pk3, tb, po, g_v, sb, rb,
    wy, wy_near, wy_full, wx, wx_near, wx_full,
    vy, vy_near, vy_full, vx, vx_near, vx_full, zs, zr,
    load_sem, psend, precv, xsend, xrecv, gsend, grecv, tsend, trecv, zsend, zrecv,
    rsend, rrecv,
):
    cut = lax.axis_index("cuts")
    dev = lax.axis_index("dev")
    count = lax.axis_size("dev")
    core = dev % 2
    x = (dev // 2) % RING
    zh = (dev // 8) % RING
    y = dev // 32
    pk = (pk0, pk1, pk2, pk3)

    def at(y_, zh_, x_, core_):
        return ((y_ * RING + zh_) * RING + x_) * 2 + core_

    partner = (cut, at(y, zh, x, 1 - core))
    x_right, x_left = (cut, at(y, zh, (x + 1) % RING, core)), (cut, at(y, zh, (x + 3) % RING, core))
    y_right, y_left = (cut, at((y + 1) % RING, zh, x, core)), (cut, at((y + 3) % RING, zh, x, core))
    to_x, to_core = place_of(x, core)
    from_x, from_core = source_of(x, core)

    def own_loads(h):
        cols = pl.ds(h * GROUP * HD, GROUP * HD)
        return (
            pltpu.make_async_copy(q_hbm.at[:, cols], q_v.at[h], load_sem.at[0, h]),
            pltpu.make_async_copy(do_hbm.at[:, cols], do_v.at[h], load_sem.at[1, h]),
        )

    def prompt_loads(h):
        return (
            pltpu.make_async_copy(
                p_hbm.at[:, pl.ds(h * HD, HD)], pk[h].at[0, 0], load_sem.at[2, h]
            ),
            pltpu.make_async_copy(
                p_hbm.at[:, pl.ds(HALF + h * HD, HD)], pk[h].at[0, 1], load_sem.at[3, h]
            ),
        )

    kv_load = pltpu.make_async_copy(kv_hbm, kv_v, load_sem.at[4, 0])

    @pl.loop(0, TILES)
    def _(t):
        cols = pl.ds(pl.multiple_of((t * 2 + core) * HD, HD), HD)
        pltpu.make_async_copy(x_hbm.at[:, cols], xo_v.at[t], load_sem.at[4, 1]).start()

    for h in range(KVH):
        for copy in prompt_loads(h) + own_loads(h):
            copy.start()
        if h == 0:
            kv_load.start()

    barrier = pltpu.get_barrier_semaphore()

    def greet(device):
        pl.semaphore_signal(
            barrier, inc=1, device_id=device, device_id_type=pl.DeviceIdType.MESH
        )

    for shift in SHIFT[1:]:
        greet((cut, (dev + shift + count) % count))
    for device in (partner, x_right, x_left, y_right, y_left):
        greet(device)
    for zl_ in range(2):
        for zh_ in range(RING):
            greet((zl_, at(y, zh_, from_x, from_core)))

    pltpu.make_async_copy(xo_v, xo_v, load_sem.at[4, 1]).wait()
    pl.semaphore_wait(barrier, 4 + 5 + 8)

    def prompt_sends(h, slot):
        device = (cut, (dev + SHIFT[slot] + count) % count)
        return (
            remote(
                p_hbm.at[:, pl.ds(h * HD, HD)], pk[h].at[slot, 0], psend.at[h], precv.at[h], device
            ),
            remote(
                p_hbm.at[:, pl.ds(HALF + h * HD, HD)], pk[h].at[slot, 1], psend.at[h], precv.at[h], device
            ),
        )

    for h in range(KVH):
        for slot in range(1, 5):
            for copy in prompt_sends(h, slot):
                copy.start()

    @pl.loop(0, TILES)
    def _(t):
        cols = pl.ds(pl.multiple_of((t * 2 + 1 - core) * HD, HD), HD)
        remote(x_hbm.at[:, cols], xp_v.at[t], xsend.at[0], xrecv.at[0], partner).start()

    @pl.loop(0, TILES)
    def _(t):
        xt_v[t, :, 0:TOK] = xo_v[t].T

    key_at = lax.broadcasted_iota(jnp.int32, (STRETCH, GROUP * STRETCH), 0)
    query_at = lax.broadcasted_iota(jnp.int32, (STRETCH, GROUP * STRETCH), 1) % STRETCH
    seen = key_at <= query_at

    def slot_of(c):
        off = off_ref[c]
        return jnp.where(off >= 0, off, REACH - off)

    def block(h, c):
        slot = slot_of(c)
        rows = pl.ds(pl.multiple_of(c * STRETCH, STRETCH), STRETCH)
        queries = jnp.concatenate(
            [q_v[h, rows, g * HD:(g + 1) * HD] for g in range(GROUP)], axis=0
        )
        dout = jnp.concatenate(
            [do_v[h, rows, g * HD:(g + 1) * HD] for g in range(GROUP)], axis=0
        )
        keys = jnp.concatenate([pk[h][slot, 0], kv_v[rows, h * HD:(h + 1) * HD]], axis=0)
        values = jnp.concatenate(
            [pk[h][slot, 1], kv_v[rows, HALF + h * HD:HALF + (h + 1) * HD]], axis=0
        )
        scores = nt(keys, queries)
        dprobs = nt(values, dout)
        scores = jnp.concatenate(
            [scores[:PLEN], jnp.where(seen, scores[PLEN:], -1e30)], axis=0
        )
        top = jnp.max(scores, axis=0, keepdims=True)
        expo = jnp.exp2((scores - top) * (SCALE * LOG2E))
        probs = expo * (1.0 / jnp.sum(expo, axis=0, keepdims=True))
        probs_b = probs.astype(BF)
        rowdot = jnp.sum(probs_b.astype(F32) * dprobs, axis=0, keepdims=True)
        dscores_b = (probs * (dprobs - rowdot)).astype(BF)
        kgrad = nn(dscores_b, queries) * SCALE
        vgrad = nn(probs_b, dout)
        g_v[h, rows, 0:HD] = kgrad[PLEN:].astype(BF)
        g_v[h, rows, HD:] = vgrad[PLEN:].astype(BF)
        tb[c, :, 0:HD] = kgrad[:PLEN]
        tb[c, :, HD:] = vgrad[:PLEN]

    def g_copy(h):
        return remote(
            g_v.at[h, pl.ds(0, TOK)], g_v.at[h, pl.ds(TOK, TOK)], gsend.at[h], grecv.at[h], partner
        )

    def term_copy(h, slot):
        device = (cut, (dev - SHIFT[slot] + count) % count)
        return remote(sb.at[h, slot - 1], rb.at[h, slot - 1], tsend.at[h], trecv.at[h], device)

    def attend(h):
        for copy in prompt_loads(h) + own_loads(h):
            copy.wait()
        if h == 0:
            kv_load.wait()
        arrived = pk[h].at[pl.ds(1, 4)]
        remote(arrived, arrived, psend.at[h], precv.at[h], partner).wait_recv()

        @pl.loop(0, BLOCKS // 2)
        def _(i):
            block(h, i * 2)
            block(h, i * 2 + 1)

        g_copy(h).start()

        slots = [slot_of(c) for c in range(BLOCKS)]

        @pl.loop(0, PLEN // 16)
        def _(i):
            rows = pl.ds(pl.multiple_of(i * 16, 16), 16)
            sums = [jnp.zeros((16, PAIR), F32) for _ in SHIFT]
            for c in range(BLOCKS):
                term = tb[c, rows]
                for n in range(len(SHIFT)):
                    sums[n] = sums[n] + jnp.where(slots[c] == n, term, 0.0)
            po[h, rows] = sums[0]
            for n in range(1, len(SHIFT)):
                sb[h, n - 1, rows] = sums[n].astype(BF)

        for slot in range(1, 5):
            term_copy(h, slot).start()

    def ring_y(h):
        return Ring(
            wy.at[h], wy_near.at[h], wy_full.at[h], rrecv.at[h, 0], rsend.at[h, 0],
            y, (y + 1) % RING, (y + 3) % RING, (y + 2) % RING, y_right, y_left,
        )

    def ring_x(h):
        return Ring(
            wx.at[h], wx_near.at[h], wx_full.at[h], rrecv.at[h, 1], rsend.at[h, 1],
            part_of(x, core), part_of((x + 1) % RING, core), part_of((x + 3) % RING, core),
            part_of((x + 2) % RING, core), x_right, x_left,
        )

    def ring_y2(h):
        return Ring(
            vx.at[h], vx_near.at[h], vx_full.at[h], rrecv.at[h, 2], rsend.at[h, 2],
            y, (y + 1) % RING, (y + 3) % RING, (y + 2) % RING, y_right, y_left,
        )

    def ring_x2(h):
        return Ring(
            vy.at[h], vy_near.at[h], vy_full.at[h], rrecv.at[h, 3], rsend.at[h, 3],
            part_of(x, core), part_of((x + 1) % RING, core), part_of((x + 3) % RING, core),
            part_of((x + 2) % RING, core), x_right, x_left,
        )

    def product(h):
        g_copy(h).wait_recv()

        def chunk(step):
            to = (y + 2 + step) % RING
            left = xt_v[pl.ds(to * RING, RING)].reshape(RING * 128, 2 * TOK)
            out = nn(left, g_v[h]).astype(BF)
            for place, z in enumerate(Z_Y):
                wy[h, to, place * 128:(place + 1) * 128] = out[z * 128:(z + 1) * 128]
            for place, z in enumerate(Z_X):
                for k in range(RING):
                    row = pl.multiple_of(to * (ROWS_X // RING) + place * 32, 32)
                    wx[h, k, pl.ds(row, 32)] = out[z * 128 + k * 32:z * 128 + (k + 1) * 32]

        chunk(0)
        ring_y(h).first()

        @pl.loop(1, RING)
        def _(step):
            chunk(step)

        ring_x(h).first()

    def second(h):
        ring_y(h).second()
        ring_x(h).second()

    def third(h):
        ring = ring_y(h)
        ring.arrive()
        for place in range(len(Z_Y)):
            for k in range(RING):
                row = place * 128 + k * 32
                vy[h, k, place * 32:(place + 1) * 32] = ring.total(pl.ds(row, 32)).astype(BF)
        ring_x2(h).first()
        ring = ring_x(h)
        ring.arrive()
        for k in range(RING):
            vx[h, k] = ring.total(pl.ds(k * (ROWS_X // RING), ROWS_X // RING)).astype(BF)
        ring_y2(h).first()

    def fourth(h):
        ring_x2(h).second()
        ring_y2(h).second()

    def z_copy(h, zl_, zh_):
        return remote(
            zs.at[h, zh_], zr.at[h, zh * 2 + cut], zsend.at[h], zrecv.at[h],
            (zl_, at(y, zh_, to_x, to_core)),
        )

    def fifth(h):
        ring = ring_x2(h)
        ring.arrive()
        for place, z in enumerate(Z_Y):
            zs[h, z] = ring.total(pl.ds(place * 32, 32)).astype(BF)
        ring = ring_y2(h)
        ring.arrive()
        for place, z in enumerate(Z_X):
            zs[h, z] = ring.total(pl.ds(place * 32, 32)).astype(BF)
        for zh_ in range(RING):
            for zl_ in range(2):
                z_copy(h, zl_, zh_).start()

    def last(h):
        remote(zr.at[h], zr.at[h], zsend.at[h], zrecv.at[h], partner).wait_recv()
        done = zr[h, 0].astype(F32)
        for source in range(1, 8):
            done = done + zr[h, source].astype(F32)
        outw_ref[:, h * HD:(h + 1) * HD] = done[:, :HD]
        outw_ref[:, HALF + h * HD:HALF + (h + 1) * HD] = done[:, HD:]

    def prompt_last(h):
        remote(rb.at[h], rb.at[h], tsend.at[h], trecv.at[h], partner).wait_recv()

        @pl.loop(0, PLEN // 32)
        def _(i):
            rows = pl.ds(pl.multiple_of(i * 32, 32), 32)
            done = po[h, rows]
            for n in range(4):
                done = done + rb[h, n, rows].astype(F32)
            outp_ref[rows, h * HD:(h + 1) * HD] = done[:, :HD]
            outp_ref[rows, HALF + h * HD:HALF + (h + 1) * HD] = done[:, HD:]

    attend(0)
    remote(xp_v, xp_v, xsend.at[0], xrecv.at[0], partner).wait_recv()

    @pl.loop(0, TILES)
    def _(t):
        xt_v[t, :, TOK:] = xp_v[t].T

    product(0)
    attend(1)
    second(0)
    product(1)
    attend(2)
    third(0)
    second(1)
    product(2)
    attend(3)
    fourth(0)
    third(1)
    second(2)
    product(3)
    fifth(0)
    fourth(1)
    third(2)
    prompt_last(0)
    second(3)
    fifth(1)
    fourth(2)
    prompt_last(1)
    third(3)
    fifth(2)
    prompt_last(2)
    last(0)
    fourth(3)
    last(1)
    prompt_last(3)
    fifth(3)
    last(2)
    last(3)

    for h in range(KVH):
        arrived = pk[h].at[pl.ds(1, 4)]
        remote(arrived, arrived, psend.at[h], precv.at[h], partner).wait_send()
        g_copy(h).wait_send()
        remote(sb.at[h], sb.at[h], tsend.at[h], trecv.at[h], partner).wait_send()
        for ring in (ring_y(h), ring_x(h), ring_x2(h), ring_y2(h)):
            ring.sent()
        remote(zr.at[h], zr.at[h], zsend.at[h], zrecv.at[h], partner).wait_send()
    remote(xp_v, xp_v, xsend.at[0], xrecv.at[0], partner).wait_send()


def shards(resp_q, resp_kv, resp_out_grad, resp_x, prompt_kv, stretch_offset):
    any_spec = pl.BlockSpec(memory_space=pl.ANY)
    vmem = pl.BlockSpec(memory_space=pltpu.VMEM)

    def ring_scratch(rows):
        return [
            pltpu.VMEM((KVH, RING, rows, PAIR), BF),
            pltpu.VMEM((KVH, 2, rows // 2, PAIR), BF),
            pltpu.VMEM((KVH, 2, rows, PAIR), BF),
        ]

    dma = pltpu.SemaphoreType.DMA
    return pl.pallas_call(
        kernel,
        out_shape=(
            jax.ShapeDtypeStruct((PLEN, KVW), F32),
            jax.ShapeDtypeStruct((32, KVW), F32),
        ),
        in_specs=[pl.BlockSpec(memory_space=pltpu.SMEM)] + [any_spec] * 5,
        out_specs=(vmem, vmem),
        scratch_shapes=[
            pltpu.VMEM((KVH, TOK, GROUP * HD), BF),
            pltpu.VMEM((KVH, TOK, GROUP * HD), BF),
            pltpu.VMEM((TOK, KVW), BF),
            pltpu.VMEM((TILES, TOK, HD), BF),
            pltpu.VMEM((TILES, TOK, HD), BF),
            pltpu.VMEM((TILES, HD, 2 * TOK), BF),
        ]
        + [pltpu.VMEM((5, 2, PLEN, HD), BF)] * KVH
        + [
            pltpu.VMEM((BLOCKS, PLEN, PAIR), F32),
            pltpu.VMEM((KVH, PLEN, PAIR), F32),
            pltpu.VMEM((KVH, 2 * TOK, PAIR), BF),
            pltpu.VMEM((KVH, 4, PLEN, PAIR), BF),
            pltpu.VMEM((KVH, 4, PLEN, PAIR), BF),
        ]
        + ring_scratch(ROWS_Y)
        + ring_scratch(ROWS_X)
        + ring_scratch(ROWS_Y // RING)
        + ring_scratch(ROWS_X // RING)
        + [
            pltpu.VMEM((KVH, RING, 32, PAIR), BF),
            pltpu.VMEM((KVH, 8, 32, PAIR), BF),
            dma((5, KVH)),
            dma((KVH,)), dma((KVH,)),
            dma((1,)), dma((1,)),
            dma((KVH,)), dma((KVH,)),
            dma((KVH,)), dma((KVH,)),
            dma((KVH,)), dma((KVH,)),
            dma((KVH, 4)), dma((KVH, 4, 4)),
        ],
        compiler_params=pltpu.CompilerParams(
            collective_id=0, has_side_effects=True, vmem_limit_bytes=56 * 1024 * 1024
        ),
        cost_estimate=pl.CostEstimate(
            flops=7_000_000_000, bytes_accessed=12_000_000, transcendentals=2_000_000
        ),
        name="attention_grads",
    )(stretch_offset, resp_q, resp_kv, resp_out_grad, resp_x, prompt_kv)


def solution(mesh):
    return jax.shard_map(
        shards,
        mesh=mesh,
        in_specs=(
            P(("cuts", "dev"), None),
            P(("cuts", "dev"), None),
            P(("cuts", "dev"), None),
            P(("cuts", "dev"), None),
            P(("cuts", "dev"), None),
            P(("cuts", "dev")),
        ),
        out_specs=(P(("cuts", "dev"), None), P("dev", None)),
        check_vma=False,
    )
```

time: 1040 us -> 91.4 us (0.09)
  waiting for transfers between devices: 771 us -> 0 us
  local copies, waits for them, and re-layouts: 185 us -> 3.45 us
  Pallas kernels: 0 us -> 86.6 us
  starting transfers between devices: 26.4 us -> 0 us
  matrix products: 24.7 us -> 0 us
  other arithmetic: 16.7 us -> 0 us
  between operations: 14.2 us -> 0.64 us
    unnamed x3 -> x0, waiting for transfers between devices: 720 us -> none
    dynamic_update_slice x8 -> x0, local copies, waits for them, and re-layouts: 120 us -> none  [shards(): lax.map(single_block, (resp_q.reshape(count, STRETCH, QH * HD), resp_kv.r...]
    pallas_call x0 -> x1, Pallas kernels: none -> 86.6 us  [shards(): pl.pallas_call(kernel, out_shape=(jax.ShapeDtypeStruct((PLEN, KVW), F32),...]
    psum x1 -> x0, waiting for transfers between devices: 41.2 us -> none  [shards(): kv_weight_grad = lax.psum(shared, 'cuts')]
    ppermute x8 -> x0, starting transfers between devices: 26.1 us -> none  [from_behind(): return lax.ppermute(value, axis, pairs)]
    dot_general x34 -> x0, matrix products: 24.7 us -> none  [the longest x1 8.22 us: shards(): lax.dot_general(resp_x, resp_grad_b, (((0,), (0,)), ((), ())), preferred_...]
    unnamed x17 -> x2, local copies, waits for them, and re-layouts: 24.2 us -> 3.45 us
    slice x18 -> x0, local copies, waits for them, and re-layouts: 17.1 us -> none  [the longest x8 7.95 us: block_terms(): chosen[:, :, half:]]
  transfers between devices with their start and end apart: 10 -> 0, of which waited for: 4 -> 0; matrix products, arithmetic and copies ran while one was open for 1% -> 0% of each run, Pallas kernels for 0% -> 0%
where the time goes in v1:
time: 91.4 us; the launch traced here: 90.7 us
  Pallas kernels  86.6 us (95%)
  local copies, waits for them, and re-layouts  3.45 us (4%)
    pallas_call x1, Pallas kernels, shards(): pl.pallas_call(kernel, out_shape=(jax.ShapeDtypeStruct((PLEN, KVW), F32),...  86.6 us
    unnamed x2, local copies, waits for them, and re-layouts  3.45 us

profile of v1, /device:TPU:1, one launch (start us, length us, event | category | flops | bytes accessed | tf_op | source)
XLA Modules:
  0.0 90.7 jit_solution(15599492790482653421)
XLA Ops:
  0.6 86.6 %attention_grads.1 = (f32[128,1024]{1,0:T(8,128)}, f32[32,1024]{1,0:T(8,128)}) custom-call(s32[8]{0:T(128)} %off_ref.1, bf16[512,2048]{1,0:T(8,128)(2,1)} %q_hbm.1, bf16[512,1024]{1,0:T(8,128)(2,1)} %kv_hbm.1, bf16[512,2048]{1,0:T(8,128)(2,1)} %do_hbm.1, bf16[512,4096]{1,0:T(8,128)(2,1)} %x_hbm.1, bf16[128,1024]{1,0:T(8,128)(2,1)} %p_hbm.1), custom_call_target="tpu_custom_call" | custom-call | flops 7000000000 | bytes 12000000 | tf_op jit(solution)/shard_map/attention_grads/pallas_call | solution.py:479
  87.2 1.9 %copy.10 = f32[128,1024]{1,0:T(8,128)} copy(f32[128,1024]{1,0:T(8,128)} %get-tuple-element.4) | data formatting | bytes 1048576
  89.1 1.6 %copy.11 = f32[32,1024]{1,0:T(8,128)} copy(f32[32,1024]{1,0:T(8,128)} %get-tuple-element.5) | data formatting | bytes 262144

commit v2 on v1

--- a/solution.py
+++ b/solution.py
@@ -21,10 +21,7 @@
 RING = 4
 TILES = 16
 PAIR = 2 * HD
-Z_Y = (0, 1, 2)
-Z_X = (3,)
-ROWS_Y = len(Z_Y) * 128
-ROWS_X = len(Z_X) * 128
+SPLIT = (((0, 1), (2, 3)),) * 4
 SHIFT = (0, 1, 2, -1, -2)
 SCALE = HD ** -0.5
 LOG2E = 1.4426950408889634
@@ -72,29 +69,29 @@
 
 
 class Ring:
-    def __init__(self, buf, near, full, far_sems, send, mine, right, left, far, to_right, to_left):
-        self.buf, self.near, self.full = buf, near, full
-        self.recv, self.send = far_sems, send
+    def __init__(self, refs, sems, mine, right, left, far, to_right, to_left):
+        self.buf, self.near, self.full = refs
+        self.recv, self.send = sems
         self.mine, self.right, self.left, self.far = mine, right, left, far
         self.to_right, self.to_left = to_right, to_left
-        self.rows = buf.shape[1]
-        self.half = self.rows // 2
+        self.half = self.buf.shape[1] // 2
 
     def copy(self, which):
         low, high = pl.ds(0, self.half), pl.ds(self.half, self.half)
-        source = (
-            self.buf.at[self.far, low],
-            self.buf.at[self.far, high],
-            self.buf.at[self.right],
-            self.buf.at[self.left],
+        source, target = (
+            (self.buf.at[self.far, low], self.near.at[0]),
+            (self.buf.at[self.far, high], self.near.at[1]),
+            (self.buf.at[self.right, high], self.full.at[0, high]),
+            (self.buf.at[self.left, low], self.full.at[1, low]),
+            (self.buf.at[self.right, low], self.full.at[0, low]),
+            (self.buf.at[self.left, high], self.full.at[1, high]),
         )[which]
-        target = (self.near if which < 2 else self.full).at[which % 2]
         device = (self.to_right, self.to_left)[which % 2]
         return remote(source, target, self.send, self.recv.at[which], device)
 
-    def first(self):
-        self.copy(0).start()
-        self.copy(1).start()
+    def start(self, *which):
+        for one in which:
+            self.copy(one).start()
 
     def second(self):
         half = self.half
@@ -102,16 +99,16 @@
         self.buf[self.right, 0:half] = (
             self.buf[self.right, 0:half].astype(F32) + self.near[0].astype(F32)
         ).astype(BF)
-        self.copy(2).start()
+        self.start(4)
         self.copy(1).wait_recv()
         self.buf[self.left, half:] = (
             self.buf[self.left, half:].astype(F32) + self.near[1].astype(F32)
         ).astype(BF)
-        self.copy(3).start()
+        self.start(5)
 
     def arrive(self):
-        self.copy(2).wait_recv()
-        self.copy(3).wait_recv()
+        for one in range(2, 6):
+            self.copy(one).wait_recv()
 
     def total(self, rows):
         return (
@@ -125,13 +122,37 @@
         remote(whole, whole, self.send, self.recv.at[0], self.to_right).wait_send()
 
 
+class Direct:
+    def __init__(self, refs, sems, mine, chunks, devices):
+        self.buf, self.full = refs
+        self.recv, self.send = sems
+        self.mine, self.chunks, self.devices = mine, chunks, devices
+
+    def first(self):
+        for step in range(3):
+            remote(
+                self.buf.at[self.chunks[step]], self.full.at[step], self.send, self.recv.at[0],
+                self.devices[step],
+            ).start()
+
+    def arrive(self):
+        remote(self.full, self.full, self.send, self.recv.at[0], self.devices[0]).wait_recv()
+
+    def total(self, rows):
+        done = self.buf[self.mine, rows].astype(F32)
+        for step in range(3):
+            done = done + self.full[step, rows].astype(F32)
+        return done
+
+    def sent(self):
+        remote(self.full, self.full, self.send, self.recv.at[0], self.devices[0]).wait_send()
+
+
 def kernel(
     off_ref, q_hbm, kv_hbm, do_hbm, x_hbm, p_hbm, outp_ref, outw_ref,
-    q_v, do_v, kv_v, xo_v, xp_v, xt_v, pk0, pk1, pk2, pk3, tb, po, g_v, sb, rb,
-    wy, wy_near, wy_full, wx, wx_near, wx_full,
-    vy, vy_near, vy_full, vx, vx_near, vx_full, zs, zr,
-    load_sem, psend, precv, xsend, xrecv, gsend, grecv, tsend, trecv, zsend, zrecv,
-    rsend, rrecv,
+    q_v, do_v, kv_v, xo_v, xp_v, xt_v, pk0, pk1, pk2, pk3, tb, po, g_v, sb, rb, cb,
+    zs, zr, load_sem, psend, precv, xsend, xrecv, gsend, grecv, tsend, trecv, zsend, zrecv,
+    rsend, rrecv, *rings,
 ):
     cut = lax.axis_index("cuts")
     dev = lax.axis_index("dev")
@@ -146,8 +167,10 @@
         return ((y_ * RING + zh_) * RING + x_) * 2 + core_
 
     partner = (cut, at(y, zh, x, 1 - core))
+    x_far, y_far = (cut, at(y, zh, (x + 2) % RING, core)), (cut, at((y + 2) % RING, zh, x, core))
     x_right, x_left = (cut, at(y, zh, (x + 1) % RING, core)), (cut, at(y, zh, (x + 3) % RING, core))
     y_right, y_left = (cut, at((y + 1) % RING, zh, x, core)), (cut, at((y + 3) % RING, zh, x, core))
+    ahead, behind = (cut, (dev + 2) % count), (cut, (dev + count - 2) % count)
     to_x, to_core = place_of(x, core)
     from_x, from_core = source_of(x, core)
 
@@ -188,37 +211,55 @@
             barrier, inc=1, device_id=device, device_id_type=pl.DeviceIdType.MESH
         )
 
-    for shift in SHIFT[1:]:
-        greet((cut, (dev + shift + count) % count))
-    for device in (partner, x_right, x_left, y_right, y_left):
+    for device in (partner, ahead, behind, x_right, x_left, x_far, y_right, y_left, y_far):
         greet(device)
     for zl_ in range(2):
         for zh_ in range(RING):
             greet((zl_, at(y, zh_, from_x, from_core)))
 
-    pltpu.make_async_copy(xo_v, xo_v, load_sem.at[4, 1]).wait()
-    pl.semaphore_wait(barrier, 4 + 5 + 8)
-
-    def prompt_sends(h, slot):
-        device = (cut, (dev + SHIFT[slot] + count) % count)
-        return (
+    pl.semaphore_wait(barrier, 9 + 8)
+
+    def prompt_copies(h, slot, device, send, recv):
+        return [
             remote(
-                p_hbm.at[:, pl.ds(h * HD, HD)], pk[h].at[slot, 0], psend.at[h], precv.at[h], device
-            ),
-            remote(
-                p_hbm.at[:, pl.ds(HALF + h * HD, HD)], pk[h].at[slot, 1], psend.at[h], precv.at[h], device
-            ),
-        )
-
+                p_hbm.at[:, pl.ds(part * HALF + h * HD, HD)], pk[h].at[slot, part],
+                psend.at[h, send], precv.at[h, recv], device,
+            )
+            for part in range(2)
+        ]
+
+    def send_far(h):
+        for copy in prompt_copies(h, 2, ahead, 0, 0) + prompt_copies(h, 4, behind, 0, 1):
+            copy.start()
+
+    def send_partner(h):
+        for copy in prompt_copies(h, 1 + 2 * core, partner, 1, 2):
+            copy.start()
+
+    def pass_copy(h):
+        return remote(
+            pk[h].at[4 - 2 * core], pk[h].at[3 - 2 * core], psend.at[h, 2], precv.at[h, 3], partner
+        )
+
+    def slot_copy(h, slot, send, recv):
+        return remote(pk[h].at[slot], pk[h].at[slot], psend.at[h, send], precv.at[h, recv], partner)
+
+    def relay(h):
+        slot_copy(h, 2, 0, 0).wait_recv()
+        slot_copy(h, 4, 0, 1).wait_recv()
+        pass_copy(h).start()
+
+    send_far(0)
     for h in range(KVH):
-        for slot in range(1, 5):
-            for copy in prompt_sends(h, slot):
-                copy.start()
+        send_partner(h)
+    send_far(1)
 
     @pl.loop(0, TILES)
     def _(t):
         cols = pl.ds(pl.multiple_of((t * 2 + 1 - core) * HD, HD), HD)
         remote(x_hbm.at[:, cols], xp_v.at[t], xsend.at[0], xrecv.at[0], partner).start()
+
+    pltpu.make_async_copy(xo_v, xo_v, load_sem.at[4, 1]).wait()
 
     @pl.loop(0, TILES)
     def _(t):
@@ -268,24 +309,44 @@
             g_v.at[h, pl.ds(0, TOK)], g_v.at[h, pl.ds(TOK, TOK)], gsend.at[h], grecv.at[h], partner
         )
 
-    def term_copy(h, slot):
-        device = (cut, (dev - SHIFT[slot] + count) % count)
-        return remote(sb.at[h, slot - 1], rb.at[h, slot - 1], tsend.at[h], trecv.at[h], device)
-
-    def attend(h):
+    def term_copies(h):
+        to_ahead = remote(sb.at[h, 3], rb.at[h, 2], tsend.at[h, 0], trecv.at[h, 2], ahead)
+        to_behind = remote(sb.at[h, 1], rb.at[h, 1], tsend.at[h, 1], trecv.at[h, 1], behind)
+        return to_ahead, to_behind
+
+    def partner_terms(h):
+        return (
+            remote(sb.at[h, 2 * core], cb.at[h], tsend.at[h, 2], trecv.at[h, 3], partner),
+            remote(sb.at[h, 2 - 2 * core], rb.at[h, 0], tsend.at[h, 3], trecv.at[h, 0], partner),
+        )
+
+    def back(h):
+        partner_terms(h)[0].wait_recv()
+        slot = 3 - 2 * core
+
+        @pl.loop(0, PLEN // 32)
+        def _(i):
+            rows = pl.ds(pl.multiple_of(i * 32, 32), 32)
+            sb[h, slot, rows] = (sb[h, slot, rows].astype(F32) + cb[h, rows].astype(F32)).astype(BF)
+
+        for copy in term_copies(h):
+            copy.start()
+
+    def ready(h):
         for copy in prompt_loads(h) + own_loads(h):
             copy.wait()
         if h == 0:
             kv_load.wait()
-        arrived = pk[h].at[pl.ds(1, 4)]
-        remote(arrived, arrived, psend.at[h], precv.at[h], partner).wait_recv()
-
-        @pl.loop(0, BLOCKS // 2)
+        slot_copy(h, 1 + 2 * core, 1, 2).wait_recv()
+        slot_copy(h, 3 - 2 * core, 2, 3).wait_recv()
+
+    def attend(h, half):
+        @pl.loop(half * 2, half * 2 + 2)
         def _(i):
             block(h, i * 2)
             block(h, i * 2 + 1)
 
-        g_copy(h).start()
+    def combine(h):
 
         slots = [slot_of(c) for c in range(BLOCKS)]
 
@@ -301,79 +362,83 @@
             for n in range(1, len(SHIFT)):
                 sb[h, n - 1, rows] = sums[n].astype(BF)
 
-        for slot in range(1, 5):
-            term_copy(h, slot).start()
+        for copy in partner_terms(h):
+            copy.start()
+
+    y_at = [(y + step) % RING for step in range(RING)]
+    x_at = [part_of((x + step) % RING, core) for step in range(RING)]
+
+    def sems(h, which):
+        return rrecv.at[h, which], rsend.at[h, which]
 
     def ring_y(h):
         return Ring(
-            wy.at[h], wy_near.at[h], wy_full.at[h], rrecv.at[h, 0], rsend.at[h, 0],
-            y, (y + 1) % RING, (y + 3) % RING, (y + 2) % RING, y_right, y_left,
+            rings[h * 10:h * 10 + 3], sems(h, 0), y_at[0], y_at[1], y_at[3], y_at[2], y_right, y_left
         )
 
     def ring_x(h):
         return Ring(
-            wx.at[h], wx_near.at[h], wx_full.at[h], rrecv.at[h, 1], rsend.at[h, 1],
-            part_of(x, core), part_of((x + 1) % RING, core), part_of((x + 3) % RING, core),
-            part_of((x + 2) % RING, core), x_right, x_left,
-        )
-
-    def ring_y2(h):
-        return Ring(
-            vx.at[h], vx_near.at[h], vx_full.at[h], rrecv.at[h, 2], rsend.at[h, 2],
-            y, (y + 1) % RING, (y + 3) % RING, (y + 2) % RING, y_right, y_left,
-        )
-
-    def ring_x2(h):
-        return Ring(
-            vy.at[h], vy_near.at[h], vy_full.at[h], rrecv.at[h, 3], rsend.at[h, 3],
-            part_of(x, core), part_of((x + 1) % RING, core), part_of((x + 3) % RING, core),
-            part_of((x + 2) % RING, core), x_right, x_left,
+            rings[h * 10 + 3:h * 10 + 6], sems(h, 1), x_at[0], x_at[1], x_at[3], x_at[2],
+            x_right, x_left,
+        )
+
+    def then_x(h):
+        return Direct(
+            rings[h * 10 + 6:h * 10 + 8], sems(h, 2), x_at[0],
+            (x_at[2], x_at[1], x_at[3]), (x_far, x_right, x_left),
+        )
+
+    def then_y(h):
+        return Direct(
+            rings[h * 10 + 8:h * 10 + 10], sems(h, 3), y_at[0],
+            (y_at[2], y_at[1], y_at[3]), (y_far, y_right, y_left),
         )
 
     def product(h):
         g_copy(h).wait_recv()
+        over_y, over_x = ring_y(h), ring_x(h)
 
         def chunk(step):
             to = (y + 2 + step) % RING
             left = xt_v[pl.ds(to * RING, RING)].reshape(RING * 128, 2 * TOK)
             out = nn(left, g_v[h]).astype(BF)
-            for place, z in enumerate(Z_Y):
-                wy[h, to, place * 128:(place + 1) * 128] = out[z * 128:(z + 1) * 128]
-            for place, z in enumerate(Z_X):
+            for place, z in enumerate(SPLIT[h][0]):
+                over_y.buf[to, place * 128:(place + 1) * 128] = out[z * 128:(z + 1) * 128]
+            rows = len(SPLIT[h][1]) * 32
+            for place, z in enumerate(SPLIT[h][1]):
                 for k in range(RING):
-                    row = pl.multiple_of(to * (ROWS_X // RING) + place * 32, 32)
-                    wx[h, k, pl.ds(row, 32)] = out[z * 128 + k * 32:z * 128 + (k + 1) * 32]
+                    row = pl.multiple_of(to * rows + place * 32, 32)
+                    over_x.buf[k, pl.ds(row, 32)] = out[z * 128 + k * 32:z * 128 + (k + 1) * 32]
 
         chunk(0)
-        ring_y(h).first()
+        over_y.start(0, 1)
 
         @pl.loop(1, RING)
         def _(step):
             chunk(step)
 
-        ring_x(h).first()
+        over_x.start(0, 1)
+        over_y.start(2, 3)
+        over_x.start(2, 3)
 
     def second(h):
         ring_y(h).second()
         ring_x(h).second()
 
     def third(h):
-        ring = ring_y(h)
+        ring, then = ring_y(h), then_x(h)
         ring.arrive()
-        for place in range(len(Z_Y)):
+        for place in range(len(SPLIT[h][0])):
             for k in range(RING):
                 row = place * 128 + k * 32
-                vy[h, k, place * 32:(place + 1) * 32] = ring.total(pl.ds(row, 32)).astype(BF)
-        ring_x2(h).first()
-        ring = ring_x(h)
+                then.buf[k, place * 32:(place + 1) * 32] = ring.total(pl.ds(row, 32)).astype(BF)
+        then.first()
+        ring, then = ring_x(h), then_y(h)
         ring.arrive()
+        rows = len(SPLIT[h][1]) * 32
         for k in range(RING):
-            vx[h, k] = ring.total(pl.ds(k * (ROWS_X // RING), ROWS_X // RING)).astype(BF)
-        ring_y2(h).first()
-
-    def fourth(h):
-        ring_x2(h).second()
-        ring_y2(h).second()
+            then.buf[k] = ring.total(pl.ds(k * rows, rows)).astype(BF)
+        then.first()
 
     def z_copy(h, zl_, zh_):
         return remote(
@@ -381,14 +446,14 @@
             (zl_, at(y, zh_, to_x, to_core)),
         )
 
-    def fifth(h):
-        ring = ring_x2(h)
+    def fourth(h):
+        ring = then_x(h)
         ring.arrive()
-        for place, z in enumerate(Z_Y):
+        for place, z in enumerate(SPLIT[h][0]):
             zs[h, z] = ring.total(pl.ds(place * 32, 32)).astype(BF)
-        ring = ring_y2(h)
+        ring = then_y(h)
         ring.arrive()
-        for place, z in enumerate(Z_X):
+        for place, z in enumerate(SPLIT[h][1]):
             zs[h, z] = ring.total(pl.ds(place * 32, 32)).astype(BF)
         for zh_ in range(RING):
             for zl_ in range(2):
@@ -403,18 +468,28 @@
         outw_ref[:, HALF + h * HD:HALF + (h + 1) * HD] = done[:, HD:]
 
     def prompt_last(h):
-        remote(rb.at[h], rb.at[h], tsend.at[h], trecv.at[h], partner).wait_recv()
+        partner_terms(h)[1].wait_recv()
+        for n in (1, 2):
+            remote(rb.at[h, n], rb.at[h, n], tsend.at[h, 0], trecv.at[h, n], partner).wait_recv()
 
         @pl.loop(0, PLEN // 32)
         def _(i):
             rows = pl.ds(pl.multiple_of(i * 32, 32), 32)
             done = po[h, rows]
-            for n in range(4):
+            for n in range(3):
                 done = done + rb[h, n, rows].astype(F32)
             outp_ref[rows, h * HD:(h + 1) * HD] = done[:, :HD]
             outp_ref[rows, HALF + h * HD:HALF + (h + 1) * HD] = done[:, HD:]
 
-    attend(0)
+    relay(0)
+    send_far(2)
+    ready(0)
+    attend(0, 0)
+    attend(0, 1)
+    g_copy(0).start()
+    relay(1)
+    send_far(3)
+    combine(0)
     remote(xp_v, xp_v, xsend.at[0], xrecv.at[0], partner).wait_recv()
 
     @pl.loop(0, TILES)
@@ -422,61 +497,86 @@
         xt_v[t, :, TOK:] = xp_v[t].T
 
     product(0)
-    attend(1)
+    back(0)
+    ready(1)
+    attend(1, 0)
+    relay(2)
+    attend(1, 1)
+    g_copy(1).start()
     second(0)
+    combine(1)
     product(1)
-    attend(2)
+    back(1)
+    ready(2)
+    attend(2, 0)
     third(0)
+    relay(3)
+    attend(2, 1)
+    g_copy(2).start()
     second(1)
+    combine(2)
     product(2)
-    attend(3)
+    back(2)
     fourth(0)
+    ready(3)
+    attend(3, 0)
     third(1)
+    attend(3, 1)
+    g_copy(3).start()
     second(2)
+    combine(3)
     product(3)
-    fifth(0)
     fourth(1)
+    back(3)
     third(2)
+    second(3)
+    fourth(2)
     prompt_last(0)
-    second(3)
-    fifth(1)
-    fourth(2)
+    third(3)
     prompt_last(1)
-    third(3)
-    fifth(2)
+    fourth(3)
     prompt_last(2)
     last(0)
-    fourth(3)
     last(1)
     prompt_last(3)
-    fifth(3)
     last(2)
     last(3)
 
     for h in range(KVH):
-        arrived = pk[h].at[pl.ds(1, 4)]
-        remote(arrived, arrived, psend.at[h], precv.at[h], partner).wait_send()
+        far = pk[h].at[pl.ds(0, 2)]
+        remote(far, far, psend.at[h, 0], precv.at[h, 0], partner).wait_send()
+        slot_copy(h, 1, 1, 2).wait_send()
+        pass_copy(h).wait_send()
         g_copy(h).wait_send()
-        remote(sb.at[h], sb.at[h], tsend.at[h], trecv.at[h], partner).wait_send()
-        for ring in (ring_y(h), ring_x(h), ring_x2(h), ring_y2(h)):
+        for copy in term_copies(h) + partner_terms(h):
+            copy.wait_send()
+        for ring in (ring_y(h), ring_x(h), then_x(h), then_y(h)):
             ring.sent()
         remote(zr.at[h], zr.at[h], zsend.at[h], zrecv.at[h], partner).wait_send()
     remote(xp_v, xp_v, xsend.at[0], xrecv.at[0], partner).wait_send()
 
 
+def hand_on(prompt_ref, weight_ref, outp_ref, outw_ref):
+    outp_ref[...] = prompt_ref[...]
+    outw_ref[...] = weight_ref[...]
+
+
 def shards(resp_q, resp_kv, resp_out_grad, resp_x, prompt_kv, stretch_offset):
     any_spec = pl.BlockSpec(memory_space=pl.ANY)
     vmem = pl.BlockSpec(memory_space=pltpu.VMEM)
 
-    def ring_scratch(rows):
-        return [
-            pltpu.VMEM((KVH, RING, rows, PAIR), BF),
-            pltpu.VMEM((KVH, 2, rows // 2, PAIR), BF),
-            pltpu.VMEM((KVH, 2, rows, PAIR), BF),
-        ]
+    def buffers(*shapes):
+        return [pltpu.VMEM(shape + (PAIR,), BF) for shape in shapes]
+
+    rings = []
+    for first_y, first_x in SPLIT:
+        for parts in (len(first_y), len(first_x)):
+            rings += buffers((RING, parts * 128), (2, parts * 64), (2, parts * 128))
+        for parts in (len(first_y), len(first_x)):
+            rings += buffers((RING, parts * 32), (3, parts * 32))
 
     dma = pltpu.SemaphoreType.DMA
-    return pl.pallas_call(
+    grads = pl.pallas_call(
         kernel,
         out_shape=(
             jax.ShapeDtypeStruct((PLEN, KVW), F32),
@@ -498,23 +598,21 @@
             pltpu.VMEM((KVH, PLEN, PAIR), F32),
             pltpu.VMEM((KVH, 2 * TOK, PAIR), BF),
             pltpu.VMEM((KVH, 4, PLEN, PAIR), BF),
-            pltpu.VMEM((KVH, 4, PLEN, PAIR), BF),
+            pltpu.VMEM((KVH, 3, PLEN, PAIR), BF),
+            pltpu.VMEM((KVH, PLEN, PAIR), BF),
         ]
-        + ring_scratch(ROWS_Y)
-        + ring_scratch(ROWS_X)
-        + ring_scratch(ROWS_Y // RING)
-        + ring_scratch(ROWS_X // RING)
         + [
             pltpu.VMEM((KVH, RING, 32, PAIR), BF),
             pltpu.VMEM((KVH, 8, 32, PAIR), BF),
             dma((5, KVH)),
-            dma((KVH,)), dma((KVH,)),
+            dma((KVH, 3)), dma((KVH, 4)),
             dma((1,)), dma((1,)),
             dma((KVH,)), dma((KVH,)),
+            dma((KVH, 4)), dma((KVH, 4)),
             dma((KVH,)), dma((KVH,)),
-            dma((KVH,)), dma((KVH,)),
-            dma((KVH, 4)), dma((KVH, 4, 4)),
-        ],
+            dma((KVH, 4)), dma((KVH, 4, 6)),
+        ]
+        + rings,
         compiler_params=pltpu.CompilerParams(
             collective_id=0, has_side_effects=True, vmem_limit_bytes=56 * 1024 * 1024
         ),
@@ -523,6 +621,16 @@
         ),
         name="attention_grads",
     )(stretch_offset, resp_q, resp_kv, resp_out_grad, resp_x, prompt_kv)
+    return pl.pallas_call(
+        hand_on,
+        out_shape=(
+            jax.ShapeDtypeStruct((PLEN, KVW), F32),
+            jax.ShapeDtypeStruct((32, KVW), F32),
+        ),
+        in_specs=[vmem, vmem],
+        out_specs=(vmem, vmem),
+        name="hand_on",
+    )(*grads)
 
 
 def solution(mesh):

time: 91.4 us -> 77.9 us (0.85)
  Pallas kernels: 86.6 us -> 76.9 us
  local copies, waits for them, and re-layouts: 3.45 us -> 0 us
    pallas_call x1, Pallas kernels: 86.6 us -> 74.9 us  [shards(): pl.pallas_call(kernel, out_shape=(jax.ShapeDtypeStruct((PLEN, KVW), F32),...]
    unnamed x2 -> x0, local copies, waits for them, and re-layouts: 3.45 us -> none
    pallas_call x0 -> x1, Pallas kernels: none -> 1.93 us  [shards(): pl.pallas_call(hand_on, out_shape=(jax.ShapeDtypeStruct((PLEN, KVW), F32)...]
where the time goes in v2:
time: 77.9 us; the launch traced here: 77.5 us
  Pallas kernels  76.9 us (99%)
    pallas_call x1, Pallas kernels, shards(): pl.pallas_call(kernel, out_shape=(jax.ShapeDtypeStruct((PLEN, KVW), F32),...  74.9 us
    pallas_call x1, Pallas kernels, shards(): pl.pallas_call(hand_on, out_shape=(jax.ShapeDtypeStruct((PLEN, KVW), F32)...  1.93 us

profile of v2, /device:TPU:1, one launch (start us, length us, event | category | flops | bytes accessed | tf_op | source)
XLA Modules:
  0.0 77.5 jit_solution(3924168925705042433)
XLA Ops:
  0.6 74.9 %attention_grads.1 = (f32[128,1024]{1,0:T(8,128)}, f32[32,1024]{1,0:T(8,128)}) custom-call(s32[8]{0:T(128)} %off_ref.1, bf16[512,2048]{1,0:T(8,128)(2,1)} %q_hbm.1, bf16[512,1024]{1,0:T(8,128)(2,1)} %kv_hbm.1, bf16[512,2048]{1,0:T(8,128)(2,1)} %do_hbm.1, bf16[512,4096]{1,0:T(8,128)(2,1)} %x_hbm.1, bf16[128,1024]{1,0:T(8,128)(2,1)} %p_hbm.1), custom_call_target="tpu_custom_call" | custom-call | flops 7000000000 | bytes 12000000 | tf_op jit(solution)/shard_map/attention_grads/pallas_call | solution.py:579
  75.6 1.9 %hand_on.1 = (f32[128,1024]{1,0:T(8,128)}, f32[32,1024]{1,0:T(8,128)}) custom-call(f32[128,1024]{1,0:T(8,128)} %get-tuple-element.4.prompt_ref, f32[32,1024]{1,0:T(8,128)} %get-tuple-element.5.weight_ref), custom_call_target="tpu_custom_call" | custom-call | tf_op jit(solution)/shard_map/hand_on/pallas_call | solution.py:624

commit v3 on v2

--- a/solution.py
+++ b/solution.py
@@ -21,7 +21,8 @@
 RING = 4
 TILES = 16
 PAIR = 2 * HD
-SPLIT = (((0, 1), (2, 3)),) * 4
+FIRST_Y = (0, 1)
+FIRST_X = (2, 3)
 SHIFT = (0, 1, 2, -1, -2)
 SCALE = HD ** -0.5
 LOG2E = 1.4426950408889634
@@ -150,7 +151,7 @@
 
 def kernel(
     off_ref, q_hbm, kv_hbm, do_hbm, x_hbm, p_hbm, outp_ref, outw_ref,
-    q_v, do_v, kv_v, xo_v, xp_v, xt_v, pk0, pk1, pk2, pk3, tb, po, g_v, sb, rb, cb,
+    q_v, do_v, kv_v, xo_v, xp_v, xt_v, pk, tb, po, g_v, sb, rb, cb,
     zs, zr, load_sem, psend, precv, xsend, xrecv, gsend, grecv, tsend, trecv, zsend, zrecv,
     rsend, rrecv, *rings,
 ):
@@ -161,7 +162,6 @@
     x = (dev // 2) % RING
     zh = (dev // 8) % RING
     y = dev // 32
-    pk = (pk0, pk1, pk2, pk3)
 
     def at(y_, zh_, x_, core_):
         return ((y_ * RING + zh_) * RING + x_) * 2 + core_
@@ -174,8 +174,23 @@
     to_x, to_core = place_of(x, core)
     from_x, from_core = source_of(x, core)
 
+    barrier = pltpu.get_barrier_semaphore()
+
+    def greet(device):
+        pl.semaphore_signal(
+            barrier, inc=1, device_id=device, device_id_type=pl.DeviceIdType.MESH
+        )
+
+    for step in (2, 1, 3, 0):
+        for zl_ in range(2):
+            greet((zl_, at(y, (zh + step) % RING, from_x, from_core)))
+    for device in (partner, ahead, behind, x_right, x_left, x_far, y_right, y_left, y_far):
+        greet(device)
+    def cols_of(h, part=0):
+        return pl.ds(pl.multiple_of(part * HALF + h * HD, HD), HD)
+
     def own_loads(h):
-        cols = pl.ds(h * GROUP * HD, GROUP * HD)
+        cols = pl.ds(pl.multiple_of(h * GROUP * HD, GROUP * HD), GROUP * HD)
         return (
             pltpu.make_async_copy(q_hbm.at[:, cols], q_v.at[h], load_sem.at[0, h]),
             pltpu.make_async_copy(do_hbm.at[:, cols], do_v.at[h], load_sem.at[1, h]),
@@ -184,75 +199,63 @@
     def prompt_loads(h):
         return (
             pltpu.make_async_copy(
-                p_hbm.at[:, pl.ds(h * HD, HD)], pk[h].at[0, 0], load_sem.at[2, h]
+                p_hbm.at[:, cols_of(h)], pk.at[h, 0, 0], load_sem.at[2, h]
             ),
             pltpu.make_async_copy(
-                p_hbm.at[:, pl.ds(HALF + h * HD, HD)], pk[h].at[0, 1], load_sem.at[3, h]
+                p_hbm.at[:, cols_of(h, 1)], pk.at[h, 0, 1], load_sem.at[3, h]
             ),
         )
 
     kv_load = pltpu.make_async_copy(kv_hbm, kv_v, load_sem.at[4, 0])
+
+    kv_load.start()
+
+    @pl.loop(0, KVH)
+    def _(h):
+        for copy in prompt_loads(h) + own_loads(h):
+            copy.start()
+
+    pl.semaphore_wait(barrier, 9 + 8)
+
+    def prompt_copies(h, slot, device, send, recv):
+        return [
+            remote(
+                p_hbm.at[:, cols_of(h, part)], pk.at[h, slot, part],
+                psend.at[h, send], precv.at[h, recv], device,
+            )
+            for part in range(2)
+        ]
+
+    def send_far(h):
+        for copy in prompt_copies(h, 2, ahead, 0, 0) + prompt_copies(h, 4, behind, 0, 1):
+            copy.start()
+
+    def send_partner(h):
+        for copy in prompt_copies(h, 1 + 2 * core, partner, 1, 2):
+            copy.start()
+
+    def pass_copy(h):
+        return remote(
+            pk.at[h, 4 - 2 * core], pk.at[h, 3 - 2 * core], psend.at[h, 2], precv.at[h, 3], partner
+        )
+
+    def slot_copy(h, slot, send, recv):
+        return remote(pk.at[h, slot], pk.at[h, slot], psend.at[h, send], precv.at[h, recv], partner)
+
+    def relay(h):
+        slot_copy(h, 2, 0, 0).wait_recv()
+        slot_copy(h, 4, 0, 1).wait_recv()
+        pass_copy(h).start()
+
+    @pl.loop(0, KVH)
+    def _(h):
+        send_far(h)
+        send_partner(h)
 
     @pl.loop(0, TILES)
     def _(t):
         cols = pl.ds(pl.multiple_of((t * 2 + core) * HD, HD), HD)
         pltpu.make_async_copy(x_hbm.at[:, cols], xo_v.at[t], load_sem.at[4, 1]).start()
-
-    for h in range(KVH):
-        for copy in prompt_loads(h) + own_loads(h):
-            copy.start()
-        if h == 0:
-            kv_load.start()
-
-    barrier = pltpu.get_barrier_semaphore()
-
-    def greet(device):
-        pl.semaphore_signal(
-            barrier, inc=1, device_id=device, device_id_type=pl.DeviceIdType.MESH
-        )
-
-    for device in (partner, ahead, behind, x_right, x_left, x_far, y_right, y_left, y_far):
-        greet(device)
-    for zl_ in range(2):
-        for zh_ in range(RING):
-            greet((zl_, at(y, zh_, from_x, from_core)))
-
-    pl.semaphore_wait(barrier, 9 + 8)
-
-    def prompt_copies(h, slot, device, send, recv):
-        return [
-            remote(
-                p_hbm.at[:, pl.ds(part * HALF + h * HD, HD)], pk[h].at[slot, part],
-                psend.at[h, send], precv.at[h, recv], device,
-            )
-            for part in range(2)
-        ]
-
-    def send_far(h):
-        for copy in prompt_copies(h, 2, ahead, 0, 0) + prompt_copies(h, 4, behind, 0, 1):
-            copy.start()
-
-    def send_partner(h):
-        for copy in prompt_copies(h, 1 + 2 * core, partner, 1, 2):
-            copy.start()
-
-    def pass_copy(h):
-        return remote(
-            pk[h].at[4 - 2 * core], pk[h].at[3 - 2 * core], psend.at[h, 2], precv.at[h, 3], partner
-        )
-
-    def slot_copy(h, slot, send, recv):
-        return remote(pk[h].at[slot], pk[h].at[slot], psend.at[h, send], precv.at[h, recv], partner)
-
-    def relay(h):
-        slot_copy(h, 2, 0, 0).wait_recv()
-        slot_copy(h, 4, 0, 1).wait_recv()
-        pass_copy(h).start()
-
-    send_far(0)
-    for h in range(KVH):
-        send_partner(h)
-    send_far(1)
 
     @pl.loop(0, TILES)
     def _(t):
@@ -282,10 +285,13 @@
         dout = jnp.concatenate(
             [do_v[h, rows, g * HD:(g + 1) * HD] for g in range(GROUP)], axis=0
         )
-        keys = jnp.concatenate([pk[h][slot, 0], kv_v[rows, h * HD:(h + 1) * HD]], axis=0)
-        values = jnp.concatenate(
-            [pk[h][slot, 1], kv_v[rows, HALF + h * HD:HALF + (h + 1) * HD]], axis=0
-        )
+        prompt = [pk[h, 0, part] for part in range(2)]
+        for n in range(1, len(SHIFT)):
+            prompt = [jnp.where(slot == n, pk[h, n, part], prompt[part]) for part in range(2)]
+        keys, values = [
+            jnp.concatenate([prompt[part], kv_v[rows, cols_of(h, part)]], axis=0)
+            for part in range(2)
+        ]
         scores = nt(keys, queries)
         dprobs = nt(values, dout)
         scores = jnp.concatenate(
@@ -335,16 +341,8 @@
     def ready(h):
         for copy in prompt_loads(h) + own_loads(h):
             copy.wait()
-        if h == 0:
-            kv_load.wait()
         slot_copy(h, 1 + 2 * core, 1, 2).wait_recv()
         slot_copy(h, 3 - 2 * core, 2, 3).wait_recv()
-
-    def attend(h, half):
-        @pl.loop(half * 2, half * 2 + 2)
-        def _(i):
-            block(h, i * 2)
-            block(h, i * 2 + 1)
 
     def combine(h):
 
@@ -368,29 +366,32 @@
     y_at = [(y + step) % RING for step in range(RING)]
     x_at = [part_of((x + step) % RING, core) for step in range(RING)]
 
+    def head(h, first, end):
+        return [ref.at[h] for ref in rings[first:end]]
+
     def sems(h, which):
         return rrecv.at[h, which], rsend.at[h, which]
 
     def ring_y(h):
         return Ring(
-            rings[h * 10:h * 10 + 3], sems(h, 0), y_at[0], y_at[1], y_at[3], y_at[2], y_right, y_left
+            head(h, 0, 3), sems(h, 0), y_at[0], y_at[1], y_at[3], y_at[2], y_right, y_left
         )
 
     def ring_x(h):
         return Ring(
-            rings[h * 10 + 3:h * 10 + 6], sems(h, 1), x_at[0], x_at[1], x_at[3], x_at[2],
+            head(h, 3, 6), sems(h, 1), x_at[0], x_at[1], x_at[3], x_at[2],
             x_right, x_left,
         )
 
     def then_x(h):
         return Direct(
-            rings[h * 10 + 6:h * 10 + 8], sems(h, 2), x_at[0],
+            head(h, 6, 8), sems(h, 2), x_at[0],
             (x_at[2], x_at[1], x_at[3]), (x_far, x_right, x_left),
         )
 
     def then_y(h):
         return Direct(
-            rings[h * 10 + 8:h * 10 + 10], sems(h, 3), y_at[0],
+            head(h, 8, 10), sems(h, 3), y_at[0],
             (y_at[2], y_at[1], y_at[3]), (y_far, y_right, y_left),
         )
 
@@ -402,20 +403,21 @@
             to = (y + 2 + step) % RING
             left = xt_v[pl.ds(to * RING, RING)].reshape(RING * 128, 2 * TOK)
             out = nn(left, g_v[h]).astype(BF)
-            for place, z in enumerate(SPLIT[h][0]):
+            for place, z in enumerate(FIRST_Y):
                 over_y.buf[to, place * 128:(place + 1) * 128] = out[z * 128:(z + 1) * 128]
-            rows = len(SPLIT[h][1]) * 32
-            for place, z in enumerate(SPLIT[h][1]):
+            rows = len(FIRST_X) * 32
+            for place, z in enumerate(FIRST_X):
                 for k in range(RING):
                     row = pl.multiple_of(to * rows + place * 32, 32)
                     over_x.buf[k, pl.ds(row, 32)] = out[z * 128 + k * 32:z * 128 + (k + 1) * 32]
 
-        chunk(0)
-        over_y.start(0, 1)
-
-        @pl.loop(1, RING)
+        @pl.loop(0, RING)
         def _(step):
             chunk(step)
+
+            @pl.when(step == 0)
+            def _():
+                over_y.start(0, 1)
 
         over_x.start(0, 1)
         over_y.start(2, 3)
@@ -428,14 +430,14 @@
     def third(h):
         ring, then = ring_y(h), then_x(h)
         ring.arrive()
-        for place in range(len(SPLIT[h][0])):
+        for place in range(len(FIRST_Y)):
             for k in range(RING):
                 row = place * 128 + k * 32
                 then.buf[k, place * 32:(place + 1) * 32] = ring.total(pl.ds(row, 32)).astype(BF)
         then.first()
         ring, then = ring_x(h), then_y(h)
         ring.arrive()
-        rows = len(SPLIT[h][1]) * 32
+        rows = len(FIRST_X) * 32
         for k in range(RING):
             then.buf[k] = ring.total(pl.ds(k * rows, rows)).astype(BF)
         then.first()
@@ -449,23 +451,23 @@
     def fourth(h):
         ring = then_x(h)
         ring.arrive()
-        for place, z in enumerate(SPLIT[h][0]):
+        for place, z in enumerate(FIRST_Y):
             zs[h, z] = ring.total(pl.ds(place * 32, 32)).astype(BF)
         ring = then_y(h)
         ring.arrive()
-        for place, z in enumerate(SPLIT[h][1]):
+        for place, z in enumerate(FIRST_X):
             zs[h, z] = ring.total(pl.ds(place * 32, 32)).astype(BF)
-        for zh_ in range(RING):
+        for step in (2, 1, 3, 0):
             for zl_ in range(2):
-                z_copy(h, zl_, zh_).start()
+                z_copy(h, zl_, (zh + step) % RING).start()
 
     def last(h):
         remote(zr.at[h], zr.at[h], zsend.at[h], zrecv.at[h], partner).wait_recv()
         done = zr[h, 0].astype(F32)
         for source in range(1, 8):
             done = done + zr[h, source].astype(F32)
-        outw_ref[:, h * HD:(h + 1) * HD] = done[:, :HD]
-        outw_ref[:, HALF + h * HD:HALF + (h + 1) * HD] = done[:, HD:]
+        outw_ref[:, cols_of(h)] = done[:, :HD]
+        outw_ref[:, cols_of(h, 1)] = done[:, HD:]
 
     def prompt_last(h):
         partner_terms(h)[1].wait_recv()
@@ -478,72 +480,69 @@
             done = po[h, rows]
             for n in range(3):
                 done = done + rb[h, n, rows].astype(F32)
-            outp_ref[rows, h * HD:(h + 1) * HD] = done[:, :HD]
-            outp_ref[rows, HALF + h * HD:HALF + (h + 1) * HD] = done[:, HD:]
+            outp_ref[rows, cols_of(h)] = done[:, :HD]
+            outp_ref[rows, cols_of(h, 1)] = done[:, HD:]
 
     relay(0)
-    send_far(2)
-    ready(0)
-    attend(0, 0)
-    attend(0, 1)
-    g_copy(0).start()
-    relay(1)
-    send_far(3)
-    combine(0)
+    kv_load.wait()
     remote(xp_v, xp_v, xsend.at[0], xrecv.at[0], partner).wait_recv()
 
     @pl.loop(0, TILES)
     def _(t):
         xt_v[t, :, TOK:] = xp_v[t].T
 
-    product(0)
-    back(0)
-    ready(1)
-    attend(1, 0)
-    relay(2)
-    attend(1, 1)
-    g_copy(1).start()
-    second(0)
-    combine(1)
-    product(1)
-    back(1)
-    ready(2)
-    attend(2, 0)
-    third(0)
-    relay(3)
-    attend(2, 1)
-    g_copy(2).start()
-    second(1)
-    combine(2)
-    product(2)
-    back(2)
-    fourth(0)
-    ready(3)
-    attend(3, 0)
-    third(1)
-    attend(3, 1)
-    g_copy(3).start()
-    second(2)
-    combine(3)
-    product(3)
-    fourth(1)
-    back(3)
-    third(2)
-    second(3)
-    fourth(2)
-    prompt_last(0)
-    third(3)
-    prompt_last(1)
-    fourth(3)
-    prompt_last(2)
-    last(0)
-    last(1)
-    prompt_last(3)
-    last(2)
-    last(3)
-
-    for h in range(KVH):
-        far = pk[h].at[pl.ds(0, 2)]
+    @pl.loop(0, KVH)
+    def _(h):
+        ready(h)
+
+        @pl.loop(0, BLOCKS // 4)
+        def _(i):
+            @pl.when((i == 1) & (h >= 2))
+            def _():
+                third(h - 2)
+
+            @pl.when((i == 1) & (h < KVH - 1))
+            def _():
+                relay(h + 1)
+
+            block(h, i * 4 + 0)
+            block(h, i * 4 + 1)
+            block(h, i * 4 + 2)
+            block(h, i * 4 + 3)
+
+        g_copy(h).start()
+
+        @pl.when(h >= 1)
+        def _():
+            second(h - 1)
+
+        combine(h)
+        product(h)
+        back(h)
+
+        @pl.when(h >= 2)
+        def _():
+            fourth(h - 2)
+
+    third(KVH - 2)
+    second(KVH - 1)
+    fourth(KVH - 2)
+
+    @pl.loop(0, KVH - 1)
+    def _(h):
+        prompt_last(h)
+
+    third(KVH - 1)
+    fourth(KVH - 1)
+    prompt_last(KVH - 1)
+
+    @pl.loop(0, KVH)
+    def _(h):
+        last(h)
+
+    @pl.loop(0, KVH)
+    def _(h):
+        far = pk.at[h, pl.ds(0, 2)]
         remote(far, far, psend.at[h, 0], precv.at[h, 0], partner).wait_send()
         slot_copy(h, 1, 1, 2).wait_send()
         pass_copy(h).wait_send()
@@ -566,14 +565,13 @@
     vmem = pl.BlockSpec(memory_space=pltpu.VMEM)
 
     def buffers(*shapes):
-        return [pltpu.VMEM(shape + (PAIR,), BF) for shape in shapes]
+        return [pltpu.VMEM((KVH,) + shape + (PAIR,), BF) for shape in shapes]
 
     rings = []
-    for first_y, first_x in SPLIT:
-        for parts in (len(first_y), len(first_x)):
-            rings += buffers((RING, parts * 128), (2, parts * 64), (2, parts * 128))
-        for parts in (len(first_y), len(first_x)):
-            rings += buffers((RING, parts * 32), (3, parts * 32))
+    for parts in (len(FIRST_Y), len(FIRST_X)):
+        rings += buffers((RING, parts * 128), (2, parts * 64), (2, parts * 128))
+    for parts in (len(FIRST_Y), len(FIRST_X)):
+        rings += buffers((RING, parts * 32), (3, parts * 32))
 
     dma = pltpu.SemaphoreType.DMA
     grads = pl.pallas_call(
@@ -591,9 +589,7 @@
             pltpu.VMEM((TILES, TOK, HD), BF),
             pltpu.VMEM((TILES, TOK, HD), BF),
             pltpu.VMEM((TILES, HD, 2 * TOK), BF),
-        ]
-        + [pltpu.VMEM((5, 2, PLEN, HD), BF)] * KVH
-        + [
+            pltpu.VMEM((KVH, 5, 2, PLEN, HD), BF),
             pltpu.VMEM((BLOCKS, PLEN, PAIR), F32),
             pltpu.VMEM((KVH, PLEN, PAIR), F32),
             pltpu.VMEM((KVH, 2 * TOK, PAIR), BF),

time: 77.9 us -> 77.5 us (level)
  no operation moved by 1% of the time
where the time goes in v3:
time: 77.5 us; the launch traced here: 77.4 us
  Pallas kernels  76.7 us (99%)
    pallas_call x1, Pallas kernels, shards(): pl.pallas_call(kernel, out_shape=(jax.ShapeDtypeStruct((PLEN, KVW), F32),...  74.8 us
    pallas_call x1, Pallas kernels, shards(): pl.pallas_call(hand_on, out_shape=(jax.ShapeDtypeStruct((PLEN, KVW), F32)...  1.93 us

profile of v3, /device:TPU:1, one launch (start us, length us, event | category | flops | bytes accessed | tf_op | source)
XLA Modules:
  0.0 77.4 jit_solution(15755598893912594684)
XLA Ops:
  0.6 74.8 %attention_grads.1 = (f32[128,1024]{1,0:T(8,128)}, f32[32,1024]{1,0:T(8,128)}) custom-call(s32[8]{0:T(128)} %off_ref.1, bf16[512,2048]{1,0:T(8,128)(2,1)} %q_hbm.1, bf16[512,1024]{1,0:T(8,128)(2,1)} %kv_hbm.1, bf16[512,2048]{1,0:T(8,128)(2,1)} %do_hbm.1, bf16[512,4096]{1,0:T(8,128)(2,1)} %x_hbm.1, bf16[128,1024]{1,0:T(8,128)(2,1)} %p_hbm.1), custom_call_target="tpu_custom_call" | custom-call | flops 7000000000 | bytes 12000000 | tf_op jit(solution)/shard_map/attention_grads/pallas_call | solution.py:577
  75.4 1.9 %hand_on.1 = (f32[128,1024]{1,0:T(8,128)}, f32[32,1024]{1,0:T(8,128)}) custom-call(f32[128,1024]{1,0:T(8,128)} %get-tuple-element.4.prompt_ref, f32[32,1024]{1,0:T(8,128)} %get-tuple-element.5.weight_ref), custom_call_target="tpu_custom_call" | custom-call | tf_op jit(solution)/shard_map/hand_on/pallas_call | solution.py:620
